TPU v7x, 256 devices: a whole 4x4x8 slice. The times are simulated.
256 devices in a mesh: item: 64 (over z, y, x_lo), user: 4 (over x_hi, core).
Axes of the slice: x: 4 (x_hi: 2, x_lo: 2; x = x_hi * 2 + x_lo), y: 4, z: 8, core: 2. Of those that a mesh axis runs over, the one named last changes fastest.
Arguments:
- query_a: bfloat16 [4096, 256], P(('item', 'user')), may hold values from -8 to 8
- query_b: bfloat16 [4096, 256], P(('item', 'user')), may hold values from -8 to 8
- items: bfloat16 [131072, 256], P('item'), may hold values from -1 to 1
- positive_a: int32 [4096], replicated, may hold values from 0 to 131071
- positive_b: int32 [4096], replicated, may hold values from 0 to 131071
- loss_cotangent: float32 [4096], replicated, may hold values from -4 to 4
Outputs:
- loss_a: float32 [4096], P(('item', 'user'))
- grad_query_b: float32 [4096, 256], P(('item', 'user'))
- grad_items: float32 [131072, 256], P(('item', 'user'))
All inputs are finite; a program needn't handle non-finite values.
Results may differ from a plain program's by a relative error of at most 0.003.
Values may be sent and summed in bfloat16 or wider, within the bound.
A program may use at most 64 MiB of HBM per device.

v0:
```python
import functools

import jax
import jax.numpy as jnp
from jax import lax
from jax.experimental import pallas as pl
from jax.experimental.pallas import tpu as pltpu
from jax.sharding import PartitionSpec as P

MESH = pl.DeviceIdType.MESH
F32 = jnp.float32
BF16 = jnp.bfloat16
HIGHEST = lax.Precision.HIGHEST

NZ, NY, NX = 8, 4, 2
OWN = 16
E = 256
GROUP = NZ * NY * NX * OWN
HALF = GROUP // NX
TILE = 512
QUARTER = 512
PIECE = 128


def remote(src, dst, send_sem, recv_sem, device):
    return pltpu.make_async_remote_copy(
        src_ref=src,
        dst_ref=dst,
        send_sem=send_sem,
        recv_sem=recv_sem,
        device_id=device,
        device_id_type=MESH,
    )


def group_row(table, selector, row_of):
    picked = jnp.dot(table, selector, precision=HIGHEST, preferred_element_type=F32)
    rows = lax.broadcasted_iota(jnp.int32, picked.shape, 0)
    return jnp.sum(jnp.where(rows == row_of, picked, 0.0), axis=0, keepdims=True)


def lse_of(parts):
    top = jnp.max(parts, axis=0)
    return top + jnp.log(jnp.sum(jnp.exp(parts - top[None]), axis=0))


def kernel(
    qa_in, qb_in, items_in, pa_in, pb_in, w_in,
    loss_hbm, gq_hbm, gi_hbm,
    items_v, items_t, qa, qb, pa_v, pb_v, w_v, pos_a, pos_b, weight,
    probs, score_a, dsc, gq_f, gq_s,
    r1, gq_h, r2,
    gi_f, gi_s, gi_core, gi_relay, gi_far, loss_out, gq_out, gi_out,
    zb, yb, za, ya,
    tops,
    in_sem, out_sem, b1_s, b1_r, b2_s, b2_r, a1_s, a1_r, a2_s, a2_r,
    b_zs, b_zr, b_ys, b_yr, a_zs, a_zr, a_ys, a_yr,
    s1s, s1r, s2s, s2r, gi_ss, gi_rs, far_s, far_r,
):
    item = lax.axis_index("item")
    user = lax.axis_index("user")
    z, y, x = item // (NY * NX), (item // NX) % NY, item % NX
    place = y * NX + x
    far, core = user // 2, user % 2
    items_rows = items_v.shape[0]
    offset = item * items_rows

    def at(zz, yy, xx):
        return {"item": (zz * NY + yy) * NX + xx}

    def z_peer(k):
        return lax.rem(z + k, NZ)

    def y_peer(k):
        return lax.rem(y + k, NY)

    def plane_peer(k):
        return lax.rem(place + k, NY * NX)

    loads = [
        pltpu.make_async_copy(source, target, in_sem.at[n])
        for n, (source, target) in enumerate(
            (
                (qb_in, qb.at[x, y, z]),
                (qa_in, qa.at[x, y, z]),
                (pa_in, pa_v),
                (pb_in, pb_v),
                (w_in, w_v),
                (items_in, items_v),
            )
        )
    ]

    barrier = pltpu.get_barrier_semaphore()

    @pl.loop(1, NZ)
    def _(k):
        pl.semaphore_signal(barrier, inc=1, device_id=at(z_peer(k), y, x), device_id_type=MESH)
        pl.semaphore_signal(barrier, inc=1, device_id=at(z_peer(k), y, 1 - x), device_id_type=MESH)

    @pl.loop(1, NY * NX)
    def _(k):
        p = plane_peer(k)
        pl.semaphore_signal(barrier, inc=1, device_id=at(z, p // NX, p % NX), device_id_type=MESH)

    other_core = {"user": far * 2 + 1 - core}
    other_far = {"item": (z * NY + y) * NX + 1 - x, "user": (1 - far) * 2 + core}
    next_x = lax.rem(far * NX + x + 1 + 2 * core, 4)
    next_chip = {"item": (z * NY + y) * NX + next_x % NX, "user": next_x // NX * 2 + core}
    pl.semaphore_signal(barrier, inc=1, device_id=other_core, device_id_type=MESH)
    pl.semaphore_signal(barrier, inc=1, device_id=other_far, device_id_type=MESH)

    for load in loads:
        load.start()

    pl.semaphore_wait(barrier, 2 * (NZ - 1) + (NY * NX - 1) + 2)

    def sent(refs, send_sem, recv_sem):
        remote(refs, refs, send_sem, recv_sem, other_core).wait_send()

    def arrived(refs, send_sem, recv_sem):
        remote(refs, refs, send_sem, recv_sem, other_core).wait_recv()

    @pl.loop(1, NZ)
    def _(k):
        remote(qb_in, qb.at[x, y, z], b1_s, b1_r, at(z_peer(k), y, x)).start()

    def gather_b_bulk():
        block = qb.at[x, y]

        @pl.loop(1, NY)
        def _(k):
            remote(block, block, b2_s, b2_r.at[x], at(z, y_peer(k), x)).start()

        @pl.loop(0, NY)
        def _(k):
            remote(block, block, b2_s, b2_r.at[x], at(z, y_peer(k), 1 - x)).start()

    @pl.loop(1, NY * NX)
    def _(k):
        p = plane_peer(k)
        remote(qa_in, qa.at[x, y, z], a1_s, a1_r, at(z, p // NX, p % NX)).start()

    def gather_a_bulk(xx):
        block = qa.at[xx, :, z]

        @pl.loop(1, NZ)
        def _(k):
            remote(block, block, a2_s, a2_r.at[xx], at(z_peer(k), y, x)).start()

    others = pl.ds(0, NZ - 1)

    lanes = lax.broadcasted_iota(jnp.int32, (1, GROUP), 1)
    own_of = lanes % OWN
    z_of = (lanes // OWN) % NZ
    y_of = (lanes // (OWN * NZ)) % NY
    x_of = lanes // (OWN * NZ * NY)
    ks = lax.broadcasted_iota(jnp.int32, (128, GROUP), 0)
    selector = (ks == x_of * (4 * OWN) + user * OWN + own_of).astype(F32)
    row_of = z_of * NY + y_of
    for load in loads[2:5]:
        load.wait()
    pos_a[...] = group_row(pa_v[...].astype(F32), selector, row_of).astype(jnp.int32) - offset
    pos_b[...] = group_row(pb_v[...].astype(F32), selector, row_of).astype(jnp.int32) - offset
    weight[...] = group_row(w_v[...], selector, row_of)

    loads[0].wait()
    arrived(qb.at[x, y, others], b1_s, b1_r)
    gather_b_bulk()
    loads[1].wait()
    arrived(qa.at[x, y, others], a1_s, a1_r)
    gather_a_bulk(x)

    loads[5].wait()
    for part in range(items_rows // QUARTER):
        rows = pl.ds(part * QUARTER, QUARTER)
        items_t[:, rows] = items_v[rows, :].T

    tiles = items_rows // TILE

    def half_of(xx):
        return pl.ds(pl.multiple_of(xx * HALF, HALF), HALF)

    def tile_of(t):
        return pl.ds(pl.multiple_of(t * TILE, TILE), TILE)

    def fold(values, op):
        return op(values.reshape(TILE // 8, 8, HALF), axis=0)

    def scores(q, xx):
        users = q[xx].reshape(HALF, E)
        return lax.dot_general(
            items_v[...], users, (((1,), (1,)), ((), ())), preferred_element_type=F32
        )

    zero = jnp.zeros((8, HALF), F32)
    least = jnp.full((8, HALF), -jnp.inf, F32)

    def half_b(xx):
        probs[xx] = scores(qb, xx)

        def largest(t, top):
            return jnp.maximum(top, fold(probs[xx, tile_of(t), :], jnp.max))

        top = jnp.max(lax.fori_loop(0, tiles, largest, least), axis=0, keepdims=True)

        def exponentials(t, total):
            p = jnp.exp(probs[xx, tile_of(t), :] - top)
            probs[xx, tile_of(t), :] = p
            return total + fold(p, jnp.sum)

        total = jnp.sum(lax.fori_loop(0, tiles, exponentials, zero), axis=0, keepdims=True)
        tops[:, half_of(xx)] = top
        zb[z, :, half_of(xx)] = top + jnp.log(total)

    def half_a(xx):
        score_a[...] = scores(qa, xx)
        pos = pos_a[:, half_of(xx)]
        ids = lax.broadcasted_iota(jnp.int32, (TILE, HALF), 0)

        def largest(t, carry):
            top, hit = carry
            score = score_a[tile_of(t), :]
            match = jnp.where(ids == pos - t * TILE, score, 0.0)
            return jnp.maximum(top, fold(score, jnp.max)), hit + fold(match, jnp.sum)

        top, hit = lax.fori_loop(0, tiles, largest, (least, zero))
        top = jnp.max(top, axis=0, keepdims=True)

        def exponentials(t, total):
            return total + fold(jnp.exp(score_a[tile_of(t), :] - top), jnp.sum)

        total = jnp.sum(lax.fori_loop(0, tiles, exponentials, zero), axis=0, keepdims=True)
        za[z, 0:1, half_of(xx)] = top + jnp.log(total)
        za[z, 1:2, half_of(xx)] = jnp.sum(hit, axis=0, keepdims=True)

    def z_round(buf, ss, rs):
        @pl.loop(1, NZ)
        def _(k):
            remote(buf.at[z], buf.at[z], ss, rs, at(z_peer(k), y, x)).start()

    def plane_round(buf, ss, rs):
        @pl.loop(1, NY * NX)
        def _(k):
            p = plane_peer(k)
            remote(buf.at[place], buf.at[place], ss, rs, at(z, p // NX, p % NX)).start()

    arrived(qb.at[x, pl.ds(0, NY - 1)], b2_s, b2_r.at[x])
    half_b(x)
    arrived(qb.at[1 - x], b2_s, b2_r.at[1 - x])
    half_b(1 - x)
    z_round(zb, b_zs, b_zr)
    gather_a_bulk(1 - x)
    sent(qb.at[x, y, others], b1_s, b1_r)
    sent(qa.at[x, y, others], a1_s, a1_r)
    sent(qb.at[0], b2_s, b2_r.at[0])
    sent(qb.at[0, pl.ds(0, NY - 1)], b2_s, b2_r.at[0])
    arrived(zb.at[others], b_zs, b_zr)
    yb[place] = lse_of(zb[...])
    plane_round(yb, b_ys, b_yr)
    arrived(qa.at[x, :, others], a2_s, a2_r.at[x])
    half_a(x)
    sent(zb.at[others], b_zs, b_zr)

    arrived(yb.at[others], b_ys, b_yr)
    factor = weight[...] * jnp.exp(tops[...] - lse_of(yb[...]))

    ids = lax.broadcasted_iota(jnp.int32, (TILE, HALF), 0)

    def dscores(ff):
        @pl.loop(ff * 2 * QUARTER // TILE, (ff + 1) * 2 * QUARTER // TILE)
        def _(t):
            for xx in range(NX):
                cols = slice(xx * HALF, (xx + 1) * HALF)
                match = jnp.where(ids == pos_b[:, cols] - t * TILE, weight[:, cols], 0.0)
                score = probs[xx, tile_of(t), :] * factor[:, cols] - match
                dsc[tile_of(t), cols] = score.astype(BF16)

    def far_copy(hop, n):
        piece = pl.ds(pl.multiple_of(n * PIECE, PIECE), PIECE)
        source, target = (gi_s, gi_relay) if hop == 0 else (gi_relay, gi_far)
        return remote(
            source.at[piece], target.at[piece], far_s.at[hop, n], far_r.at[hop, n], next_chip
        )

    def core_copy(n):
        return remote(gi_f.at[n, 1 - core], gi_core.at[n], gi_ss.at[n], gi_rs.at[n], other_core)

    def item_grads(n, ff):
        rows = pl.ds(pl.multiple_of(ff * (2 * QUARTER), 2 * QUARTER), 2 * QUARTER)
        part = jnp.dot(dsc[rows, :], qb[...].reshape(GROUP, E), preferred_element_type=F32)
        gi_f[n] = part.reshape(2, QUARTER, E)
        core_copy(n).start()

    def query_grads(xx):
        block = jnp.dot(
            items_t[...], dsc[:, xx * HALF : (xx + 1) * HALF], preferred_element_type=F32
        ).T.reshape(NY, NZ, OWN, E)
        gq_f[xx] = block
        gq_s[xx] = block.astype(BF16)

        @pl.loop(1, NY)
        def _(k):
            yy = y_peer(k)
            remote(gq_s.at[xx, yy], r1.at[place], s1s, s1r, at(z, yy, xx)).start()

        @pl.when(x != xx)
        def _():
            remote(gq_s.at[xx, y], r1.at[place], s1s, s1r, at(z, y, xx)).start()

    dscores(1 - far)
    item_grads(0, 1 - far)
    dscores(far)
    query_grads(0)
    core_copy(0).wait_recv()
    gi_s[...] = (gi_f[0, core] + gi_core[0]).astype(BF16)

    @pl.loop(0, QUARTER // PIECE)
    def _(n):
        far_copy(0, n).start()

    query_grads(1)
    item_grads(1, far)

    arrived(qa.at[1 - x, :, others], a2_s, a2_r.at[1 - x])
    half_a(1 - x)
    z_round(za, a_zs, a_zr)

    @pl.loop(0, QUARTER // PIECE)
    def _(n):
        far_copy(0, n).wait_recv()
        far_copy(1, n).start()

    r1[place] = jnp.zeros((NZ, OWN, E), BF16)
    r2[z] = jnp.zeros((OWN, E), F32)
    arrived(r1.at[others], s1s, s1r)
    gq_h[...] = gq_f[x, y] + jnp.sum(r1[...].astype(F32), axis=0)

    @pl.loop(1, NZ)
    def _(k):
        zz = z_peer(k)
        remote(gq_h.at[zz], r2.at[z], s2s, s2r, at(zz, y, x)).start()

    arrived(za.at[others], a_zs, a_zr)
    z_parts = za[...]
    ya[place, 0:1] = lse_of(z_parts[:, 0:1])
    ya[place, 1:2] = jnp.sum(z_parts[:, 1:2], axis=0)
    plane_round(ya, a_ys, a_yr)

    core_copy(1).wait_recv()
    gi_out[...] = gi_f[1, core] + gi_core[1]
    sent(qa.at[0, :, others], a2_s, a2_r.at[0])
    sent(qa.at[1, :, others], a2_s, a2_r.at[0])
    sent(yb.at[others], b_ys, b_yr)
    sent(za.at[others], a_zs, a_zr)
    sent(r1.at[others], s1s, s1r)
    core_copy(0).wait_send()
    core_copy(1).wait_send()

    @pl.loop(0, QUARTER // PIECE)
    def _(n):
        far_copy(0, n).wait_send()

    @pl.loop(0, QUARTER // PIECE)
    def _(n):
        piece = pl.ds(pl.multiple_of(n * PIECE, PIECE), PIECE)
        far_copy(1, n).wait_recv()
        gi_out[piece, :] += gi_far[piece, :].astype(F32)

    stores = [
        pltpu.make_async_copy(source, target, out_sem.at[n])
        for n, (source, target) in enumerate(
            ((gi_out, gi_hbm), (loss_out, loss_hbm), (gq_out, gq_hbm))
        )
    ]
    stores[0].start()

    arrived(ya.at[others], a_ys, a_yr)
    y_parts = ya[...]
    tops[...] = lse_of(y_parts[:, 0:1]) - jnp.sum(y_parts[:, 1:2], axis=0)
    mine = tops[:, pl.ds(pl.multiple_of((x * NY + y) * NZ * OWN, NZ * OWN), NZ * OWN)]
    pick_row = lax.broadcasted_iota(jnp.int32, (NZ * OWN, OWN), 0)
    pick_col = lax.broadcasted_iota(jnp.int32, (NZ * OWN, OWN), 1)
    pick = (pick_row == z * OWN + pick_col).astype(F32)
    loss_out[...] = jnp.dot(mine, pick, precision=HIGHEST, preferred_element_type=F32)
    stores[1].start()

    arrived(r2.at[others], s2s, s2r)
    gq_out[...] = gq_h[z] + jnp.sum(r2[...], axis=0)
    stores[2].start()

    sent(ya.at[others], a_ys, a_yr)
    sent(r2.at[others], s2s, s2r)

    @pl.loop(0, QUARTER // PIECE)
    def _(n):
        far_copy(1, n).wait_send()

    for store in stores:
        store.wait()


def hand_over(*refs):
    sources, targets, held, (in_sem, out_sem) = refs[:3], refs[3:6], refs[6:9], refs[9:]
    ways = list(zip(sources, held, targets))
    steps = QUARTER // PIECE
    parts = [tuple(r.at[pl.ds(n * PIECE, PIECE)] for r in ways[2]) for n in range(steps)]
    parts = parts + ways[:2]
    reads = [
        pltpu.make_async_copy(source, middle, in_sem.at[n])
        for n, (source, middle, target) in enumerate(parts)
    ]
    writes = [
        pltpu.make_async_copy(middle, target, out_sem.at[n])
        for n, (source, middle, target) in enumerate(parts)
    ]
    for read in reads:
        read.start()
    for read, write in zip(reads, writes):
        read.wait()
        write.start()
    for write in writes:
        write.wait()


def per_device(query_a, query_b, items, positive_a, positive_b, loss_cotangent):
    rows = items.shape[0]
    hbm = pl.BlockSpec(memory_space=pl.ANY)
    results = (
        jax.ShapeDtypeStruct((1, OWN), F32),
        jax.ShapeDtypeStruct((OWN, E), F32),
        jax.ShapeDtypeStruct((QUARTER, E), F32),
    )
    dma = pltpu.SemaphoreType.DMA
    block = (NX, NY, NZ, OWN, E)
    loss, gq, gi = pl.pallas_call(
        kernel,
        out_shape=results,
        in_specs=[hbm] * 6,
        out_specs=[hbm] * 3,
        scratch_shapes=[
            pltpu.VMEM((rows, E), BF16),
            pltpu.VMEM((E, rows), BF16),
            pltpu.VMEM(block, BF16),
            pltpu.VMEM(block, BF16),
            pltpu.VMEM((32, 128), jnp.int32),
            pltpu.VMEM((32, 128), jnp.int32),
            pltpu.VMEM((32, 128), F32),
            pltpu.VMEM((1, GROUP), jnp.int32),
            pltpu.VMEM((1, GROUP), jnp.int32),
            pltpu.VMEM((1, GROUP), F32),
            pltpu.VMEM((NX, rows, HALF), F32),
            pltpu.VMEM((rows, HALF), F32),
            pltpu.VMEM((rows, GROUP), BF16),
            pltpu.VMEM(block, F32),
            pltpu.VMEM(block, BF16),
            pltpu.VMEM((NY * NX, NZ, OWN, E), BF16),
            pltpu.VMEM((NZ, OWN, E), F32),
            pltpu.VMEM((NZ, OWN, E), F32),
            pltpu.VMEM((2, 2, QUARTER, E), F32),
            pltpu.VMEM((QUARTER, E), BF16),
            pltpu.VMEM((2, QUARTER, E), F32),
            pltpu.VMEM((QUARTER, E), BF16),
            pltpu.VMEM((QUARTER, E), BF16),
            pltpu.VMEM((1, OWN), F32),
            pltpu.VMEM((OWN, E), F32),
            pltpu.VMEM((QUARTER, E), F32),
            pltpu.VMEM((NZ, 1, GROUP), F32),
            pltpu.VMEM((NY * NX, 1, GROUP), F32),
            pltpu.VMEM((NZ, 2, GROUP), F32),
            pltpu.VMEM((NY * NX, 2, GROUP), F32),
            pltpu.VMEM((1, GROUP), F32),
            dma((6,)),
            dma((3,)),
            dma, dma,
            dma, dma((NX,)),
            dma, dma,
            dma, dma((NX,)),
            dma, dma,
            dma, dma,
            dma, dma,
            dma, dma,
            dma, dma,
            dma, dma,
            dma((2,)), dma((2,)),
            dma((2, QUARTER // PIECE)), dma((2, QUARTER // PIECE)),
        ],
        compiler_params=pltpu.CompilerParams(
            collective_id=0, has_side_effects=True, vmem_limit_bytes=64 * 1024 * 1024
        ),
    )(
        query_a,
        query_b,
        items,
        positive_a.reshape(32, 128),
        positive_b.reshape(32, 128),
        loss_cotangent.reshape(32, 128),
    )
    pieces = QUARTER // PIECE + 2
    loss, gq, gi = pl.pallas_call(
        hand_over,
        out_shape=results,
        in_specs=[hbm] * 3,
        out_specs=[hbm] * 3,
        scratch_shapes=[pltpu.VMEM(r.shape, r.dtype) for r in results] + [dma((pieces,))] * 2,
        compiler_params=pltpu.CompilerParams(vmem_limit_bytes=64 * 1024 * 1024),
    )(loss, gq, gi)
    return loss.reshape(OWN), gq, gi


def solution(mesh):
    return jax.shard_map(
        per_device,
        mesh=mesh,
        in_specs=(
            P(("item", "user"), None),
            P(("item", "user"), None),
            P("item", None),
            P(),
            P(),
            P(),
        ),
        out_specs=(P(("item", "user")), P(("item", "user"), None), P(("item", "user"), None)),
        check_vma=False,
    )
```

profile of v0, /device:TPU:2, one launch (start us, length us, event | category | flops | bytes accessed | tf_op | source)
XLA Modules:
  0.0 56.5 jit_solution(2096179534079095764)
XLA Ops:
  0.6 54.0 %shard_map.85 = (f32[1,16]{1,0:T(1,128)}, f32[16,256]{1,0:T(8,128)}, f32[512,256]{1,0:T(8,128)}) custom-call(bf16[16,256]{1,0:T(8,128)(2,1)} %qa_in.1, bf16[16,256]{1,0:T(8,128)(2,1)} %qb_in.1, bf16[2048,256]{1,0:T(8,128)(2,1)} %items_in.1, s32[32,128]{1,0:T(8,128)} %bitcast.4, s32[32,128]{1,0:T(8,128)} %bitcast.5, f32[32,128]{1,0:T(8,128)} %bitcast.6), custom_call_target="tpu_custom_call" | custom-call | tf_op jit(solution)/shard_map/pallas_call | solution.py:436
  54.6 1.9 %shard_map.86 = (f32[1,16]{1,0:T(1,128)}, f32[16,256]{1,0:T(8,128)}, f32[512,256]{1,0:T(8,128)}) custom-call(f32[1,16]{1,0:T(1,128)} %get-tuple-element.9.refs_0_, f32[16,256]{1,0:T(8,128)} %get-tuple-element.10.refs_1_, f32[512,256]{1,0:T(8,128)} %get-tuple-element.11.refs_2_), custom_call_target="tpu_custom_call" | custom-call | tf_op jit(solution)/shard_map/pallas_call | solution.py:500
where the time goes:
time: 57.3 us; the launch traced here: 56.5 us
  Pallas kernels  55.9 us (98%)
  between operations  0.64 us (1%)
    pallas_call x1, Pallas kernels, per_device(): pl.pallas_call(kernel, out_shape=results, in_specs=[hbm] * 6, out_specs=[...  54 us
    pallas_call x1, Pallas kernels, per_device(): pl.pallas_call(hand_over, out_shape=results, in_specs=[hbm] * 3, out_spec...  1.86 us

commit v1 on v0

--- a/solution.py
+++ b/solution.py
@@ -267,14 +267,17 @@
 
     ids = lax.broadcasted_iota(jnp.int32, (TILE, HALF), 0)
 
-    def dscores(ff):
-        @pl.loop(ff * 2 * QUARTER // TILE, (ff + 1) * 2 * QUARTER // TILE)
-        def _(t):
-            for xx in range(NX):
-                cols = slice(xx * HALF, (xx + 1) * HALF)
-                match = jnp.where(ids == pos_b[:, cols] - t * TILE, weight[:, cols], 0.0)
-                score = probs[xx, tile_of(t), :] * factor[:, cols] - match
-                dsc[tile_of(t), cols] = score.astype(BF16)
+    def quarter_of(ff, cc):
+        return pl.ds(pl.multiple_of((ff * 2 + cc) * QUARTER, QUARTER), QUARTER)
+
+    def dscores(ff, cc):
+        rows = quarter_of(ff, cc)
+        for xx in range(NX):
+            cols = slice(xx * HALF, (xx + 1) * HALF)
+            match = jnp.where(
+                ids == pos_b[:, cols] - (ff * 2 + cc) * QUARTER, weight[:, cols], 0.0
+            )
+            dsc[rows, cols] = (probs[xx, rows, :] * factor[:, cols] - match).astype(BF16)
 
     def far_copy(hop, n):
         piece = pl.ds(pl.multiple_of(n * PIECE, PIECE), PIECE)
@@ -286,15 +289,14 @@
     def core_copy(n):
         return remote(gi_f.at[n, 1 - core], gi_core.at[n], gi_ss.at[n], gi_rs.at[n], other_core)
 
-    def item_grads(n, ff):
-        rows = pl.ds(pl.multiple_of(ff * (2 * QUARTER), 2 * QUARTER), 2 * QUARTER)
-        part = jnp.dot(dsc[rows, :], qb[...].reshape(GROUP, E), preferred_element_type=F32)
-        gi_f[n] = part.reshape(2, QUARTER, E)
-        core_copy(n).start()
+    def item_grads(n, ff, cc):
+        gi_f[n, cc] = jnp.dot(
+            dsc[quarter_of(ff, cc), :], qb[...].reshape(GROUP, E), preferred_element_type=F32
+        )
 
     def query_grads(xx):
         block = jnp.dot(
-            items_t[...], dsc[:, xx * HALF : (xx + 1) * HALF], preferred_element_type=F32
+            items_t[...], dsc[:, half_of(xx)], preferred_element_type=F32
         ).T.reshape(NY, NZ, OWN, E)
         gq_f[xx] = block
         gq_s[xx] = block.astype(BF16)
@@ -308,10 +310,14 @@
         def _():
             remote(gq_s.at[xx, y], r1.at[place], s1s, s1r, at(z, y, xx)).start()
 
-    dscores(1 - far)
-    item_grads(0, 1 - far)
-    dscores(far)
-    query_grads(0)
+    dscores(1 - far, 1 - core)
+    item_grads(0, 1 - far, 1 - core)
+    core_copy(0).start()
+    dscores(1 - far, core)
+    item_grads(0, 1 - far, core)
+    dscores(far, 1 - core)
+    dscores(far, core)
+    query_grads(1 - x)
     core_copy(0).wait_recv()
     gi_s[...] = (gi_f[0, core] + gi_core[0]).astype(BF16)
 
@@ -319,8 +325,10 @@
     def _(n):
         far_copy(0, n).start()
 
-    query_grads(1)
-    item_grads(1, far)
+    query_grads(x)
+    item_grads(1, far, 1 - core)
+    core_copy(1).start()
+    item_grads(1, far, core)
 
     arrived(qa.at[1 - x, :, others], a2_s, a2_r.at[1 - x])
     half_a(1 - x)

time: 57.3 us -> 55.5 us (0.969)
  Pallas kernels: 55.9 us -> 54 us
    pallas_call x1, Pallas kernels: 54 us -> 52.1 us  [per_device(): pl.pallas_call(kernel, out_shape=results, in_specs=[hbm] * 6, out_specs=[...]
where the time goes in v1:
time: 55.5 us; the launch traced here: 54.6 us
  Pallas kernels  54 us (97%)
  between operations  0.64 us (1%)
    pallas_call x1, Pallas kernels, per_device(): pl.pallas_call(kernel, out_shape=results, in_specs=[hbm] * 6, out_specs=[...  52.1 us
    pallas_call x1, Pallas kernels, per_device(): pl.pallas_call(hand_over, out_shape=results, in_specs=[hbm] * 3, out_spec...  1.86 us

profile of v1, /device:TPU:2, one launch (start us, length us, event | category | flops | bytes accessed | tf_op | source)
XLA Modules:
  0.0 54.6 jit_solution(13602402696769315534)
XLA Ops:
  0.6 52.1 %shard_map.85 = (f32[1,16]{1,0:T(1,128)}, f32[16,256]{1,0:T(8,128)}, f32[512,256]{1,0:T(8,128)}) custom-call(bf16[16,256]{1,0:T(8,128)(2,1)} %qa_in.1, bf16[16,256]{1,0:T(8,128)(2,1)} %qb_in.1, bf16[2048,256]{1,0:T(8,128)(2,1)} %items_in.1, s32[32,128]{1,0:T(8,128)} %bitcast.4, s32[32,128]{1,0:T(8,128)} %bitcast.5, f32[32,128]{1,0:T(8,128)} %bitcast.6), custom_call_target="tpu_custom_call" | custom-call | tf_op jit(solution)/shard_map/pallas_call | solution.py:444
  52.7 1.9 %shard_map.86 = (f32[1,16]{1,0:T(1,128)}, f32[16,256]{1,0:T(8,128)}, f32[512,256]{1,0:T(8,128)}) custom-call(f32[1,16]{1,0:T(1,128)} %get-tuple-element.9.refs_0_, f32[16,256]{1,0:T(8,128)} %get-tuple-element.10.refs_1_, f32[512,256]{1,0:T(8,128)} %get-tuple-element.11.refs_2_), custom_call_target="tpu_custom_call" | custom-call | tf_op jit(solution)/shard_map/pallas_call | solution.py:508
